TPU v7x, 32 devices: a whole 2x2x4 slice. The times are simulated.
32 devices in a mesh: groups: 2 (over y), wide: 4 (over x, core), tp: 4 (over z).
Axes of the slice: x: 2, y: 2, z: 4, core: 2. Of those that a mesh axis runs over, the one named last changes fastest.
Arguments:
- queries: bfloat16 [256, 8192], P(('groups', 'wide'), 'tp'), parts along dimension 0, may hold values from -26 to 26
- cached_key_rows: bfloat16 [256, 8, 256, 128], P(('groups', 'wide'), 'tp'), parts along dimension 0, may hold values from -16 to 16
- cached_value_rows: bfloat16 [256, 8, 256, 128], P(('groups', 'wide'), 'tp'), parts along dimension 0, may hold values from -6 to 6
- fresh_token_key: bfloat16 [256, 1024], P(('groups', 'wide'), 'tp'), parts along dimension 0, may hold values from -6 to 6
- fresh_token_value: bfloat16 [256, 1024], P(('groups', 'wide'), 'tp'), parts along dimension 0, may hold values from -6 to 6
- lengths: int32 [256], P(('groups', 'wide')), parts along dimension 0, may hold values from 1 to 256, 16384 in all
- residual: bfloat16 [256, 8192], P(('groups', 'wide'), 'tp'), parts along dimension 0, may hold values from -13 to 13
- norm_gain_vector: bfloat16 [8192], P('tp'), may hold values from 0.25 to 1.75
- gate_matrix: bfloat16 [8192, 16384], P('tp', 'wide'), may hold values from -0.0625 to 0.0625
- up_matrix: bfloat16 [8192, 16384], P('tp', 'wide'), may hold values from -0.0625 to 0.0625
- down_matrix: bfloat16 [16384, 8192], P('wide', 'tp'), may hold values from -0.046875 to 0.046875
- adapter_input_maps: bfloat16 [32, 8192, 32], P(('groups', 'wide'), 'tp'), parts along dimension 0, may hold values from -0.0625 to 0.0625
- adapter_output_maps: bfloat16 [32, 32, 16384], P('groups', 'tp', 'wide'), parts along dimension 0, may hold values from -1.5 to 1.5
- down_adapter_input: bfloat16 [32, 16, 16384], P('groups', None, ('wide', 'tp')), parts along dimension 0, may hold values from -0.046875 to 0.046875
- down_adapter_output: bfloat16 [32, 16, 8192], P(('groups', 'wide'), None, 'tp'), parts along dimension 0, may hold values from -1.5 to 1.5
- request_adapter: int32 [256], P('groups'), parts along dimension 0, may hold values from 0 to 15
- adapter_storage_slot: int32 [32], P('groups'), parts along dimension 0, may hold values from 0 to 15, each once
Outputs:
- layer_out: bfloat16 [256, 8192], P(('groups', 'wide'), 'tp'), parts along dimension 0
There are 2 independent parts, one for each index of `groups`. A program takes and returns all parts, laid end to end along the dimension named above; an argument that names none is the same for every part. Nothing has to cross between parts.
Inputs may be any that keep to these rules, and one draw needn't show every extreme that they name: `adapter_storage_slot`: a permutation of the slots. The 128 lengths of each group sum to 16384, and some request of each group fills its whole cache.
All inputs are finite; a program needn't handle non-finite values.
Results may differ from a plain program's by a relative error of at most 0.014.
Values may be sent and summed in bfloat16 or wider, within the bound.
A program may use at most 192 MiB of HBM per device.

v0:
```python
import math

import jax
import jax.numpy as jnp
from jax import lax
from jax.sharding import PartitionSpec as P


def per_device(
    queries,
    cached_key_rows,
    cached_value_rows,
    fresh_token_key,
    fresh_token_value,
    lengths,
    residual,
    norm_gain_vector,
    gate_matrix,
    up_matrix,
    down_matrix,
    adapter_input_maps,
    adapter_output_maps,
    down_adapter_input,
    down_adapter_output,
    request_adapter,
    adapter_storage_slot,
):
    rows_here = queries.shape[0]
    kv_here = cached_key_rows.shape[1]
    context = cached_key_rows.shape[2]
    head_size = cached_key_rows.shape[3]
    group_size = queries.shape[1] // (kv_here * head_size)
    score_scale = 1.0 / math.sqrt(head_size)
    query_heads = queries.reshape(rows_here, kv_here, group_size, head_size)
    scores = (
        jnp.einsum(
            "rkgd,rkld->rkgl", query_heads, cached_key_rows, preferred_element_type=jnp.float32
        )
        * score_scale
    )
    own_score = (
        jnp.einsum(
            "rkgd,rkd->rkg",
            query_heads,
            fresh_token_key.reshape(rows_here, kv_here, head_size),
            preferred_element_type=jnp.float32,
        )
        * score_scale
    )
    visible = lax.broadcasted_iota(jnp.int32, (rows_here, context), 1) < lengths[:, None]
    scores = jnp.where(visible[:, None, None, :], scores, jnp.float32(-1e30))
    row_peak = jnp.maximum(jnp.max(scores, axis=-1), own_score)
    weights = jnp.exp(scores - row_peak[..., None])
    own_weight = jnp.exp(own_score - row_peak)
    denominator = jnp.sum(weights, axis=-1) + own_weight
    fresh_value = fresh_token_value.reshape(rows_here, kv_here, head_size).astype(jnp.float32)
    mixed = jnp.einsum(
        "rkgl,rkld->rkgd",
        weights.astype(jnp.bfloat16),
        cached_value_rows,
        preferred_element_type=jnp.float32,
    )
    mixed = mixed + own_weight[..., None] * fresh_value[:, :, None, :]
    attn = (mixed / denominator[..., None]).reshape(rows_here, -1).astype(jnp.bfloat16)
    stream = (residual.astype(jnp.float32) + attn.astype(jnp.float32)).astype(jnp.bfloat16)
    tp_count = lax.axis_size("tp")
    my_tp = lax.axis_index("tp")
    my_wide = lax.axis_index("wide")
    width_portion = residual.shape[1]
    as_float = stream.astype(jnp.float32)
    square_sum = lax.psum(jnp.sum(as_float * as_float, axis=1, keepdims=True), "tp")
    mean_square = square_sum / jnp.float32(width_portion * tp_count)
    normed = (
        as_float * lax.rsqrt(mean_square + 1e-05) * norm_gain_vector.astype(jnp.float32)[None, :]
    ).astype(jnp.bfloat16)
    owned_number = adapter_input_maps.shape[0]
    adapter_number = adapter_output_maps.shape[0]
    rank_portion = adapter_output_maps.shape[1]
    adapter_rank_size = down_adapter_input.shape[1]
    hidden_portion = gate_matrix.shape[1]
    subset_width = down_adapter_input.shape[2]
    every_request_row = request_adapter.shape[0]
    adapter_ids = lax.broadcasted_iota(jnp.int32, (every_request_row, adapter_number), 1)
    adapter_hits = request_adapter[:, None] == adapter_ids
    slot_of_row = jnp.sum(jnp.where(adapter_hits, adapter_storage_slot[None, :], 0), axis=1)
    slot_hits = slot_of_row[:, None] == adapter_ids
    owned_ids = my_wide * owned_number + lax.broadcasted_iota(
        jnp.int32, (every_request_row, owned_number), 1
    )
    local_hits = slot_of_row[:, None] == owned_ids
    inner_lookup = jnp.transpose(adapter_input_maps, (1, 0, 2)).reshape(
        width_portion, owned_number * 2 * adapter_rank_size
    )
    block_rows = lax.all_gather(normed, "wide", axis=0, tiled=True)
    request_number = block_rows.shape[0]
    gate_part = jnp.dot(block_rows, gate_matrix, preferred_element_type=jnp.float32)
    up_part = jnp.dot(block_rows, up_matrix, preferred_element_type=jnp.float32)
    inner_all = jnp.dot(block_rows, inner_lookup, preferred_element_type=jnp.float32).reshape(
        request_number, owned_number, 2 * adapter_rank_size
    )
    inner_part = jnp.sum(jnp.where(local_hits[:, :, None], inner_all, jnp.float32(0.0)), axis=1)
    joined = jnp.concatenate([gate_part, up_part, inner_part], axis=1)
    inner_sum = lax.psum(joined[:, 2 * hidden_portion :], ("wide", "tp"))
    inner_low = inner_sum.astype(jnp.bfloat16)
    positioned = jnp.where(slot_hits[:, :, None], inner_low[:, None, :], jnp.bfloat16(0.0))
    rank_start = my_tp * rank_portion
    placed_slice = lax.dynamic_slice_in_dim(positioned, rank_start, rank_portion, 2)
    rank_position = rank_start + lax.broadcasted_iota(jnp.int32, (rank_portion,), 0)
    gate_select_mask = rank_position < adapter_rank_size
    gate_input = jnp.where(
        gate_select_mask[None, None, :], placed_slice, jnp.bfloat16(0.0)
    ).reshape(every_request_row, adapter_number * rank_portion)
    up_input = jnp.where(gate_select_mask[None, None, :], jnp.bfloat16(0.0), placed_slice).reshape(
        every_request_row, adapter_number * rank_portion
    )
    output_lookup = adapter_output_maps.reshape(adapter_number * rank_portion, hidden_portion)
    gate_pre = joined[:, :hidden_portion] + jnp.dot(
        gate_input, output_lookup, preferred_element_type=jnp.float32
    )
    up_pre = joined[:, hidden_portion : 2 * hidden_portion] + jnp.dot(
        up_input, output_lookup, preferred_element_type=jnp.float32
    )
    gate_total, up_total = lax.psum((gate_pre, up_pre), "tp")
    hidden_state = (jax.nn.silu(gate_total) * up_total).astype(jnp.bfloat16)
    hidden_subset = lax.dynamic_slice_in_dim(hidden_state, my_tp * subset_width, subset_width, 1)
    down_gathered = lax.dot_general(
        hidden_subset,
        down_adapter_input,
        (((1,), (2,)), ((), ())),
        preferred_element_type=jnp.float32,
    )
    down_part = jnp.sum(jnp.where(slot_hits[:, :, None], down_gathered, jnp.float32(0.0)), axis=1)
    down_low = lax.psum(down_part, ("wide", "tp")).astype(jnp.bfloat16)
    local_positioned = jnp.where(local_hits[:, :, None], down_low[:, None, :], jnp.bfloat16(0.0))
    adapter_change = jnp.dot(
        local_positioned.reshape(every_request_row, owned_number * adapter_rank_size),
        down_adapter_output.reshape(owned_number * adapter_rank_size, width_portion),
        preferred_element_type=jnp.float32,
    )
    product = jnp.dot(hidden_state, down_matrix, preferred_element_type=jnp.float32)
    projected = lax.psum_scatter(product, "wide", scatter_dimension=0, tiled=True)
    projected = projected + lax.psum_scatter(
        adapter_change, "wide", scatter_dimension=0, tiled=True
    )
    return (stream.astype(jnp.float32) + projected).astype(jnp.bfloat16)


def solution(mesh):
    return jax.shard_map(
        per_device,
        mesh=mesh,
        in_specs=(
            P(("groups", "wide"), "tp"),
            P(("groups", "wide"), "tp", None, None),
            P(("groups", "wide"), "tp", None, None),
            P(("groups", "wide"), "tp"),
            P(("groups", "wide"), "tp"),
            P(("groups", "wide")),
            P(("groups", "wide"), "tp"),
            P("tp"),
            P("tp", "wide"),
            P("tp", "wide"),
            P("wide", "tp"),
            P(("groups", "wide"), "tp", None),
            P("groups", "tp", "wide"),
            P("groups", None, ("wide", "tp")),
            P(("groups", "wide"), None, "tp"),
            P("groups"),
            P("groups"),
        ),
        out_specs=P(("groups", "wide"), "tp"),
        check_vma=False,
    )
```

profile of v0, /device:TPU:0, one launch (start us, length us, event | category | flops | bytes accessed | tf_op | source)
XLA Modules:
  0.0 350.8 jit_solution(11987299424548842127)
XLA Ops:
  6.6 0.8 select_reduce_fusion
  7.5 0.7 iota_compare_fusion
  8.2 0.7 convert_element_type.60
  8.9 0.7 reshape.111
  9.6 0.7 reshape.101
  10.4 0.9 copy.25
  11.5 3.6 %fusion.42 = (f32[32,2,8]{2,1,0:T(2,128)S(1)}, f32[32,2,8,256]{3,2,1,0:T(8,128)S(1)}) fusion(bf16[32,2,8,128]{3,2,1,0:T(8,128)(2,1)S(1)} %bitcast.56, bf16[32,2,256,128]{3,2,1,0:T(8,128)(2,1)} %param.18, pred[32,256]{1,0:T(8,128)(4,1)S(1)} %iota_compare_fusion), kind=kOutput, calls=%fused_computation.66 | convolution fusion | flops 33947136 | bytes 4859904 | tf_op jit(solution)/shard_map/rkgd,rkld->rkgl/dot_general | solution.py:36
  15.6 0.7 fusion.6
  16.6 13.5 %psum.35 = f32[32,1]{0,1:T(1,128)S(1)} all-reduce(f32[32,1]{0,1:T(1,128)S(1)} %bitcast.61), channel_id=1, replica_groups=mesh['groups'=2,'wide'=4,'tp'=4] {'tp'}, use_global_device_ids=true, to_apply=%region_3.4 | all-reduce | flops 32 | bytes 256 | tf_op jit(solution)/shard_map/psum | solution.py:71
  30.2 7.2 %all_gather.3 = bf16[128,2048]{1,0:T(8,128)(2,1)S(1)} all-gather(bf16[32,2048]{1,0:T(8,128)(2,1)S(1)} %fusion.17), channel_id=1, replica_groups=mesh['groups'=2,'wide'=4,'tp'=4] {'wide'}, dimensions={0}, use_global_device_ids=true | all-gather | bytes 655360 | tf_op jit(solution)/shard_map/all_gather | solution.py:94
  37.4 0.3 fusion.8
  37.7 58.0 %psum.36 = bf16[128,32]{0,1:T(8,128)(2,1)S(1)} all-reduce(f32[128,32]{0,1:T(8,128)S(1)} %fusion.8), channel_id=1, replica_groups=mesh['groups'=2,'wide'=4,'tp'=4] {'wide','tp'}, use_global_device_ids=true, to_apply=%region_6.7 | all-reduce | flops 4096 | bytes 24576 | tf_op jit(solution)/shard_map/psum | solution.py:103
  95.6 9.5 %fusion.45 = f32[128,4096]{1,0:T(8,128)} fusion(bf16[128,2048]{1,0:T(8,128)(2,1)S(1)} %all_gather.3, bf16[2048,4096]{1,0:T(8,128)(2,1)} %param.26), kind=kOutput, calls=%fused_computation.69 | convolution fusion | flops 2147483648 | bytes 19398656 | tf_op jit(solution)/shard_map/dot_general | solution.py:97
  105.1 9.5 %fusion.44 = f32[128,4096]{1,0:T(8,128)} fusion(bf16[128,2048]{1,0:T(8,128)(2,1)S(1)} %all_gather.3, bf16[2048,4096]{1,0:T(8,128)(2,1)} %param.25), kind=kOutput, calls=%fused_computation.68 | convolution fusion | flops 2147483648 | bytes 19398656 | tf_op jit(solution)/shard_map/dot_general | solution.py:96
  114.6 4.0 %fusion.1 = f32[128,4096]{1,0:T(8,128)} fusion(f32[128,4096]{1,0:T(8,128)} %fusion.45, bf16[16,8,4096]{2,1,0:T(8,128)(2,1)S(1)} %copy-done, pred[8]{0:T(512)(128)(4,1)S(1)} %add_compare_fusion, pred[128,16]{0,1:T(8,128)(4,1)S(1)} %iota_compare_fusion.1, bf16[128,8]{0,1:T(8,128)(2,1)S(1)} %constant_dynamic-slice_fusion), kind=kOutput, calls=%fused_computation.3 | convolution fusion | flops 134774784 | bytes 5246984 | tf_op jit(solution)/shard_map/dot_general | solution.py:120
  118.6 2.3 fusion
  120.9 153.3 %all-reduce.3.cloned.1.call-done = (f32[128,4096]{1,0:T(8,128)}, f32[128,4096]{1,0:T(8,128)}) async-done(((f32[128,4096]{1,0:T(8,128)}, f32[128,4096]{1,0:T(8,128)}), (f32[128,4096]{1,0:T(8,128)}, f32[128,4096]{1,0:T(8,128)})) %all-reduce.3.cloned.1.call-update) | async-done | bytes 4194320 | tf_op jit(solution)/shard_map/psum | solution.py:123
  274.2 2.9 multiply_convert_fusion
  277.0 0.3 fusion.7
  277.4 32.5 %psum.39 = bf16[128,16]{0,1:T(8,128)(2,1)S(1)} all-reduce(f32[128,16]{0,1:T(8,128)S(1)} %fusion.7), channel_id=1, replica_groups=mesh['groups'=2,'wide'=4,'tp'=4] {'wide','tp'}, use_global_device_ids=true, to_apply=%region_11.12 | all-reduce | flops 2048 | bytes 12288 | tf_op jit(solution)/shard_map/psum | solution.py:133
  309.9 8.1 %fusion.46 = f32[128,2048]{1,0:T(8,128)S(1)} fusion(bf16[128,4096]{1,0:T(8,128)(2,1)S(1)} %multiply_convert_fusion, bf16[4096,2048]{1,0:T(8,128)(2,1)} %param.27), kind=kOutput, calls=%fused_computation.70 | convolution fusion | flops 2147483648 | bytes 18874368 | tf_op jit(solution)/shard_map/dot_general | solution.py:140
  318.1 1.3 fusion.2
  319.4 22.8 %reduce-scatter.2.cloned.1.call-done = f32[32,2048]{1,0:T(8,128)} async-done(((f32[128,2048]{1,0:T(8,128)}), f32[32,2048]{1,0:T(8,128)}) %reduce-scatter.2.cloned.1.call-update) | async-done | bytes 262160 | tf_op jit(solution)/shard_map/reduce_scatter | solution.py:141
  342.3 1.6 fusion.18
  (30 shorter events, 1.2 us)
Async XLA Ops:
  6.5 108.0 %copy-start = (bf16[16,8,4096]{2,1,0:T(8,128)(2,1)S(1)}, bf16[16,8,4096]{2,1,0:T(8,128)(2,1)}, u32[]{:S(2)}) copy-start(bf16[16,8,4096]{2,1,0:T(8,128)(2,1)} %param.29) | copy-start | bytes 3145732
  6.5 267.6 %all-reduce.3.cloned.1.call-start = ((), (), s32[]{:S(2)}) async-start(), calls=%async_computation.2 | async-start | bytes 8388608 | tf_op jit(solution)/shard_map/psum | solution.py:123
  11.5 4.0 %copy-start.5 = (bf16[32,2,256,128]{3,2,1,0:T(8,128)(2,1)S(1)}, bf16[32,2,256,128]{3,2,1,0:T(8,128)(2,1)}, u32[]{:S(2)}) copy-start(bf16[32,2,256,128]{3,2,1,0:T(8,128)(2,1)} %param.19) | copy-start | bytes 12582916
  15.5 0.9 copy-start.4
  15.5 21.8 %copy-start.2 = (bf16[4,2048,32]{1,2,0:T(8,128)(2,1)S(1)}, bf16[4,2048,32]{1,2,0:T(8,128)(2,1)}, u32[]{:S(2)}) copy-start(bf16[4,2048,32]{1,2,0:T(8,128)(2,1)} %param.28) | copy-start | bytes 1572868
  114.6 4.0 %copy-start.1 = (f32[128,4096]{1,0:T(8,128)S(1)}, f32[128,4096]{1,0:T(8,128)}, u32[]{:S(2)}) copy-start(f32[128,4096]{1,0:T(8,128)} %fusion.44) | copy-start | bytes 6291460
  120.9 221.4 %reduce-scatter.2.cloned.1.call-start = ((), (), s32[]{:S(2)}) async-start(), calls=%async_computation.1 | async-start | bytes 1310720 | tf_op jit(solution)/shard_map/reduce_scatter | solution.py:141
  274.2 2.9 copy-start.6
  309.9 8.2 %copy-start.3 = (bf16[4,16,2048]{2,1,0:T(8,128)(2,1)S(1)}, bf16[4,16,2048]{2,1,0:T(8,128)(2,1)}, u32[]{:S(2)}) copy-start(bf16[4,16,2048]{2,1,0:T(8,128)(2,1)} %param.31) | copy-start | bytes 786436
Sparse Core Ops, SparseCore 0:
  121.0 153.1 all-reduce.2
  319.6 22.6 reduce-scatter.1
where the time goes:
time: 351 us
  waiting for transfers between devices  176 us (50%)
  blocking collectives  111 us (32%)
  matrix products  39.8 us (11%)
  between operations  13.6 us (4%)
  other arithmetic  7.48 us (2%)
    psum x1, waiting for transfers between devices, per_device(): gate_total, up_total = lax.psum((gate_pre, up_pre), 'tp')  153 us
    psum x1, blocking collectives, per_device(): inner_sum = lax.psum(joined[:, 2 * hidden_portion:], ('wide', 'tp'))  58 us
    psum x1, blocking collectives, per_device(): down_low = lax.psum(down_part, ('wide', 'tp')).astype(jnp.bfloat16)  32.5 us
    reduce_scatter x1, waiting for transfers between devices, per_device(): lax.psum_scatter(product, 'wide', scatter_dimension=0, tiled=True)  22.8 us
    psum x1, blocking collectives, per_device(): lax.psum(jnp.sum(as_float * as_float, axis=1, keepdims=True), 'tp')  13.5 us
    dot_general x1, matrix products, per_device(): jnp.dot(block_rows, gate_matrix, preferred_element_type=jnp.float32)  9.46 us
    dot_general x1, matrix products, per_device(): up_part = jnp.dot(block_rows, up_matrix, preferred_element_type=jnp.float32)  9.46 us
    dot_general x1, matrix products, per_device(): jnp.dot(hidden_state, down_matrix, preferred_element_type=jnp.float32)  8.14 us
  transfers between devices with their start and end apart: 2, of which 2 were waited for; matrix products, arithmetic and copies ran while one was open for 0% of the time, Pallas kernels for 0%

commit v1 on v0

--- a/solution.py
+++ b/solution.py
@@ -3,7 +3,346 @@
 import jax
 import jax.numpy as jnp
 from jax import lax
+from jax.experimental import pallas as pl
+from jax.experimental.pallas import tpu as pltpu
 from jax.sharding import PartitionSpec as P
+
+MESH = pl.DeviceIdType.MESH
+NT = (((1,), (1,)), ((), ()))
+TN = (((0,), (0,)), ((), ()))
+
+
+def feed_forward_kernel(
+    slot_ref, stream_ref, gain_ref, ain_hbm, omap_hbm, dai_hbm, dout_hbm, gate_hbm, up_hbm, down_hbm,
+    out_ref,
+    raw, x, ain, omap, dai, dout, w, dw,
+    ex_send, ex_recv, pf, s1_send, s1_recv, fwd, own, s2_send, s2_recv,
+    hid, dinner, dx_send, dx_recv, acc, o_send, o_recv,
+    small_sem, w_sem, dw_sem,
+    raw_ss, raw_rs, ex_ss, ex_rs, s1_ss, s1_rs, s2_ss, s2_rs, h_ss, h_rs, dx_ss, dx_rs, o_ss, o_rs,
+):
+    f32, bf16 = jnp.float32, jnp.bfloat16
+    rows, width = stream_ref.shape
+    total = 4 * rows
+    sub = w.shape[2] // 2
+    me_w, z = lax.axis_index("wide"), lax.axis_index("tp")
+    me = me_w * 4 + z
+    z1 = z + 1 - 2 * lax.rem(z, 2)
+    z2 = lax.rem(z + 2, 4)
+    z3 = 3 - z
+    quarters = (z3, z2, z1, z)
+
+    def column(q, b):
+        return pl.multiple_of((q * 4 + b) * sub, sub)
+
+    def w_copy(slot, b, i, start):
+        half, parts = slot * 4 + i, []
+        for j, src in enumerate((gate_hbm, up_hbm)):
+            parts.append(pltpu.make_async_copy(
+                src.at[:, pl.ds(column(quarters[i], b), sub)],
+                w.at[half, :, pl.ds(j * sub, sub)], w_sem.at[half, j]))
+        for part in parts:
+            part.start() if start else part.wait()
+
+    def dw_copy(k):
+        return pltpu.make_async_copy(
+            down_hbm.at[pl.ds(pl.multiple_of(k * sub, sub), sub), :], dw.at[k], dw_sem.at[k])
+
+    def small_copy(j):
+        src, dst = ((ain_hbm, ain), (omap_hbm, omap), (dai_hbm, dai), (dout_hbm, dout))[j]
+        return pltpu.make_async_copy(src, dst, small_sem.at[j])
+
+    def remote(src, dst, ss, rs, dev_w, dev_t):
+        return pltpu.make_async_remote_copy(
+            src_ref=src, dst_ref=dst, send_sem=ss, recv_sem=rs,
+            device_id={"wide": dev_w, "tp": dev_t}, device_id_type=MESH)
+
+    barrier = pltpu.get_barrier_semaphore()
+
+    def greet(e, carry):
+        peer = lax.rem(me + e, 16)
+        pl.semaphore_signal(barrier, inc=1, device_id={"wide": peer // 4, "tp": lax.rem(peer, 4)},
+                            device_id_type=MESH)
+        return carry
+
+    lax.fori_loop(1, 16, greet, 0)
+    small_copy(0).start()
+    for slot in range(2):
+        for i in range(4):
+            w_copy(slot, slot, i, True)
+        if slot == 0:
+            small_copy(1).start()
+    small_copy(2).start()
+    small_copy(3).start()
+    raw[me_w] = stream_ref[...]
+    pl.semaphore_wait(barrier, 15)
+
+    def raw_copy(owner, d, dev):
+        return remote(raw.at[owner], raw.at[owner], raw_ss.at[d - 1], raw_rs.at[owner], dev, z)
+
+    for d in (1, 2, 3):
+        raw_copy(me_w, d, lax.rem(me_w + d, 4)).start()
+
+    def dw_start(k, carry):
+        dw_copy(k).start()
+        return carry
+
+    lax.fori_loop(0, 16, dw_start, 0)
+    for d in (1, 2, 3):
+        peer = lax.rem(me_w + d, 4)
+        raw_copy(peer, d, peer).wait_recv()
+    gain = gain_ref[...].astype(f32)
+    squares = []
+    for p in range(4):
+        part = raw[p].astype(f32)
+        squares.append(jnp.sum(part * part, axis=1, keepdims=True))
+        x[pl.ds(p * rows, rows), :] = (part * gain).astype(bf16)
+    square = jnp.broadcast_to(jnp.concatenate(squares, axis=0), (total, total)).T
+
+    slot_row = slot_ref[...]
+    small_copy(0).wait()
+    inner = lax.dot_general(ain[...], x[...], NT, preferred_element_type=f32)
+    chosen = jnp.zeros((32, total), f32)
+    for a in range(4):
+        chosen = chosen + jnp.where(slot_row == me_w * 4 + a, inner[a * 32:(a + 1) * 32], 0.0)
+    for t in range(4):
+        ex_send[t, 0:8, :] = chosen[t * 8:(t + 1) * 8]
+        ex_send[t, 8:16, :] = square[0:8]
+
+    def ex_start(e, carry):
+        peer = lax.rem(me + e, 16)
+        pt = lax.rem(peer, 4)
+        remote(ex_send.at[pt], ex_recv.at[me], ex_ss.at[e], ex_rs.at[me], peer // 4, pt).start()
+        return carry
+
+    lax.fori_loop(1, 16, ex_start, 0)
+    ex_recv[me] = ex_send[z]
+
+    def fill(b):
+        slot = lax.rem(b, 2)
+        for i in range(4):
+            w_copy(slot, b, i, False)
+            pf[i] = jnp.dot(x[...], w[slot * 4 + i], preferred_element_type=f32)
+
+        @pl.when(b < 2)
+        def _():
+            for i in range(4):
+                w_copy(slot, b + 2, i, True)
+
+    fill(jnp.int32(0))
+
+    def ex_wait(e, carry):
+        peer = lax.rem(me + e, 16)
+        desc = remote(ex_send.at[z], ex_recv.at[peer], ex_ss.at[e], ex_rs.at[peer], peer // 4, lax.rem(peer, 4))
+        desc.wait_recv()
+        desc.wait_send()
+        return carry
+
+    lax.fori_loop(1, 16, ex_wait, 0)
+    low = ex_recv[0, 0:8, :]
+    for e in range(1, 16):
+        low = low + ex_recv[e, 0:8, :]
+    square = ex_recv[me_w * 4, 8:16, :]
+    for t in range(1, 4):
+        square = square + ex_recv[me_w * 4 + t, 8:16, :]
+    scale_row = lax.rsqrt(square / f32(width * 4) + 1e-05)
+    scale = jnp.broadcast_to(scale_row[0:1], (total, total)).T
+    scale = jnp.concatenate([scale] * (sub // total), axis=1)
+    placed = jnp.concatenate([jnp.where(slot_row == a, low, 0.0) for a in range(16)], axis=0).T.astype(bf16)
+    is_gate = z < 2
+    small_copy(1).wait()
+
+    def s1_copy(j, b):
+        return remote(s1_send.at[j, b], s1_recv.at[j, b], s1_ss.at[j, b], s1_rs.at[j, b], me_w, z1)
+
+    def s2_copy(b):
+        return remote(s2_send.at[b], s2_recv.at[b], s2_ss.at[b], s2_rs.at[b], me_w, z2)
+
+    def pass_on(b):
+        s1_copy(0, b).wait_recv()
+        s2_send[b] = (fwd[b] + s1_recv[0, b].astype(f32)).astype(bf16)
+        s2_copy(b).start()
+
+    def spread(b, carry):
+        for i in range(4):
+            term = jnp.dot(placed, omap[:, pl.ds(column(quarters[i], b), sub)], preferred_element_type=f32)
+            value = pf[i] + jnp.concatenate(
+                [jnp.where(is_gate, term, 0.0), jnp.where(is_gate, 0.0, term)], axis=1)
+            if i == 1:
+                fwd[b] = value
+            elif i == 3:
+                own[b] = value
+            else:
+                s1_send[i // 2, b] = value.astype(bf16)
+                s1_copy(i // 2, b).start()
+
+        @pl.when(b < 3)
+        def _():
+            fill(b + 1)
+
+        @pl.when(b > 0)
+        def _():
+            pass_on(b - 1)
+
+        return carry
+
+    lax.fori_loop(0, 4, spread, 0)
+    pass_on(jnp.int32(3))
+
+    def h_copy(q, b, d, dev):
+        return remote(hid.at[q, b], hid.at[q, b], h_ss.at[d - 1, b], h_rs.at[q, b], me_w, dev)
+
+    def add_product(q, b):
+        k = q * 4 + b
+        dw_copy(k).wait()
+        acc[...] += jnp.dot(hid[q, b], dw[k], preferred_element_type=f32)
+
+    def add_others(b):
+        for d in (1, 2, 3):
+            q = quarters[3 - d]
+            h_copy(q, b, d, q).wait_recv()
+            add_product(q, b)
+
+    acc[...] = jnp.zeros_like(acc)
+    dinner[...] = jnp.zeros_like(dinner)
+    small_copy(2).wait()
+
+    def finish(b, carry):
+        s1_copy(1, b).wait_recv()
+        s2_copy(b).wait_recv()
+        value = own[b] + s1_recv[1, b].astype(f32) + s2_recv[b].astype(f32)
+        gate = value[:, :sub] * scale
+        up = value[:, sub:] * scale
+        hid[z, b] = (gate / (1.0 + jnp.exp(-gate)) * up).astype(bf16)
+        for d in (3, 2, 1):
+            h_copy(z, b, d, quarters[3 - d]).start()
+        dinner[...] += lax.dot_general(
+            dai[:, pl.ds(pl.multiple_of(b * sub, sub), sub)], hid[z, b], NT, preferred_element_type=f32)
+        add_product(z, b)
+
+        @pl.when(b > 0)
+        def _():
+            add_others(b - 1)
+
+        return carry
+
+    lax.fori_loop(0, 4, finish, 0)
+
+    down_low = jnp.zeros((16, total), f32)
+    for a in range(16):
+        down_low = down_low + jnp.where(slot_row == a, dinner[a * 16:(a + 1) * 16, :], 0.0)
+    dx_send[...] = down_low
+    dx_recv[me] = down_low
+
+    def dx_copy(owner, e, peer):
+        return remote(dx_send, dx_recv.at[owner], dx_ss.at[e], dx_rs.at[owner], peer // 4, lax.rem(peer, 4))
+
+    def dx_start(e, carry):
+        dx_copy(me, e, lax.rem(me + e, 16)).start()
+        return carry
+
+    lax.fori_loop(1, 16, dx_start, 0)
+    add_others(jnp.int32(3))
+
+    def dx_wait(e, carry):
+        peer = lax.rem(me + e, 16)
+        dx_copy(peer, e, peer).wait_recv()
+        dx_copy(peer, e, peer).wait_send()
+        return carry
+
+    lax.fori_loop(1, 16, dx_wait, 0)
+    down_low = dx_recv[0]
+    for e in range(1, 16):
+        down_low = down_low + dx_recv[e]
+    placed_down = jnp.concatenate(
+        [jnp.where(slot_row == me_w * 4 + a, down_low, 0.0) for a in range(4)], axis=0).astype(bf16)
+    small_copy(3).wait()
+    acc[...] += lax.dot_general(placed_down, dout[...], TN, preferred_element_type=f32)
+
+    def o_copy(d, dev):
+        return remote(o_send.at[d - 1], o_recv.at[d - 1], o_ss.at[d - 1], o_rs.at[d - 1], dev, z)
+
+    for d in (2, 3, 1):
+        peer = lax.rem(me_w + d, 4)
+        o_send[d - 1] = acc[pl.ds(pl.multiple_of(peer * rows, rows), rows), :].astype(bf16)
+        o_copy(d, peer).start()
+    result = stream_ref[...].astype(f32) + acc[pl.ds(pl.multiple_of(me_w * rows, rows), rows), :]
+    for d in (1, 2, 3):
+        o_copy(d, lax.rem(me_w + d, 4)).wait_recv()
+        result = result + o_recv[d - 1].astype(f32)
+    out_ref[...] = result.astype(bf16)
+
+    for d in (1, 2, 3):
+        peer = lax.rem(me_w + d, 4)
+        raw_copy(me_w, d, peer).wait_send()
+        o_copy(d, peer).wait_send()
+
+    def drain(b, carry):
+        s1_copy(0, b).wait_send()
+        s1_copy(1, b).wait_send()
+        s2_copy(b).wait_send()
+        for d in (1, 2, 3):
+            h_copy(z, b, d, quarters[3 - d]).wait_send()
+        return carry
+
+    lax.fori_loop(0, 4, drain, 0)
+
+
+def feed_forward(stream, norm_gain, gate, up, down, ain, omaps, dai, dout, slot_of_row):
+    rows, width = stream.shape
+    total = 4 * rows
+    hidden = gate.shape[1]
+    sub = hidden // 16
+    owned, _, rank2 = ain.shape
+    f32, bf16 = jnp.float32, jnp.bfloat16
+    ain_t = jnp.transpose(ain, (0, 2, 1)).reshape(owned * rank2, width)
+    omap = omaps.reshape(omaps.shape[0] * omaps.shape[1], hidden)
+    dai2 = dai.reshape(dai.shape[0] * dai.shape[1], dai.shape[2])
+    dout2 = dout.reshape(dout.shape[0] * dout.shape[1], width)
+    dma = pltpu.SemaphoreType.DMA
+    vmem = pl.BlockSpec(memory_space=pltpu.VMEM)
+    hbm = pl.BlockSpec(memory_space=pl.ANY)
+    return pl.pallas_call(
+        feed_forward_kernel,
+        out_shape=jax.ShapeDtypeStruct((rows, width), bf16),
+        in_specs=[vmem] * 3 + [hbm] * 7,
+        out_specs=vmem,
+        scratch_shapes=[
+            pltpu.VMEM((4, rows, width), bf16),
+            pltpu.VMEM((total, width), bf16),
+            pltpu.VMEM(ain_t.shape, bf16),
+            pltpu.VMEM(omap.shape, bf16),
+            pltpu.VMEM(dai2.shape, bf16),
+            pltpu.VMEM(dout2.shape, bf16),
+            pltpu.VMEM((8, width, 2 * sub), bf16),
+            pltpu.VMEM((16, sub, width), bf16),
+            pltpu.VMEM((4, 16, total), f32),
+            pltpu.VMEM((16, 16, total), f32),
+            pltpu.VMEM((4, total, 2 * sub), f32),
+            pltpu.VMEM((2, 4, total, 2 * sub), bf16),
+            pltpu.VMEM((2, 4, total, 2 * sub), bf16),
+            pltpu.VMEM((4, total, 2 * sub), f32),
+            pltpu.VMEM((4, total, 2 * sub), f32),
+            pltpu.VMEM((4, total, 2 * sub), bf16),
+            pltpu.VMEM((4, total, 2 * sub), bf16),
+            pltpu.VMEM((4, 4, total, sub), bf16),
+            pltpu.VMEM((dai2.shape[0], total), f32),
+            pltpu.VMEM((16, total), f32),
+            pltpu.VMEM((16, 16, total), f32),
+            pltpu.VMEM((total, width), f32),
+            pltpu.VMEM((3, rows, width), bf16),
+            pltpu.VMEM((3, rows, width), bf16),
+            dma((4,)), dma((8, 2)), dma((16,)),
+            dma((3,)), dma((4,)), dma((16,)), dma((16,)),
+            dma((2, 4)), dma((2, 4)), dma((4,)), dma((4,)),
+            dma((3, 4)), dma((4, 4)), dma((16,)), dma((16,)), dma((3,)), dma((3,)),
+        ],
+        compiler_params=pltpu.CompilerParams(
+            collective_id=0, has_side_effects=True, vmem_limit_bytes=58 * 2**20),
+        cost_estimate=pl.CostEstimate(
+            flops=6 * total * width * hidden, bytes_accessed=6 * width * hidden, transcendentals=0),
+    )(slot_of_row.reshape(1, total), stream, norm_gain.reshape(1, width), ain_t, omap, dai2, dout2,
+      gate, up, down)
 
 
 def per_device(
@@ -63,6 +402,25 @@
     mixed = mixed + own_weight[..., None] * fresh_value[:, :, None, :]
     attn = (mixed / denominator[..., None]).reshape(rows_here, -1).astype(jnp.bfloat16)
     stream = (residual.astype(jnp.float32) + attn.astype(jnp.float32)).astype(jnp.bfloat16)
+    if lax.axis_size("tp") == 4 and lax.axis_size("wide") == 4 and rows_here == 32:
+        ids = lax.broadcasted_iota(
+            jnp.int32, (request_adapter.shape[0], adapter_storage_slot.shape[0]), 1
+        )
+        slots = jnp.sum(
+            jnp.where(request_adapter[:, None] == ids, adapter_storage_slot[None, :], 0), axis=1
+        )
+        return feed_forward(
+            stream,
+            norm_gain_vector,
+            gate_matrix,
+            up_matrix,
+            down_matrix,
+            adapter_input_maps,
+            adapter_output_maps,
+            down_adapter_input,
+            down_adapter_output,
+            slots,
+        )
     tp_count = lax.axis_size("tp")
     my_tp = lax.axis_index("tp")
     my_wide = lax.axis_index("wide")

time: 351 us -> 105 us (0.30)
  waiting for transfers between devices: 176 us -> 0 us
  blocking collectives: 111 us -> 0 us
  Pallas kernels: 0 us -> 92.3 us
  matrix products: 39.8 us -> 6.57 us
  between operations: 13.6 us -> 0.12 us
  other arithmetic: 7.48 us -> 2.51 us
    psum x1 -> x0, waiting for transfers between devices: 153 us -> none  [per_device(): gate_total, up_total = lax.psum((gate_pre, up_pre), 'tp')]
    psum x3 -> x0, blocking collectives: 104 us -> none  [the longest x1 58 us: per_device(): inner_sum = lax.psum(joined[:, 2 * hidden_portion:], ('wide', 'tp'))]
    pallas_call x0 -> x1, Pallas kernels: none -> 92.3 us  [feed_forward(): pl.pallas_call(feed_forward_kernel, out_shape=jax.ShapeDtypeStruct((rows,...]
    dot_general x8 -> x0, matrix products: 35.2 us -> none  [the longest x1 9.46 us: per_device(): jnp.dot(block_rows, gate_matrix, preferred_element_type=jnp.float32)]
    reduce_scatter x1 -> x0, waiting for transfers between devices: 22.8 us -> none  [per_device(): lax.psum_scatter(product, 'wide', scatter_dimension=0, tiled=True)]
    all_gather x1 -> x0, blocking collectives: 7.17 us -> none  [per_device(): block_rows = lax.all_gather(normed, 'wide', axis=0, tiled=True)]
    convert_element_type x4 -> x1, other arithmetic: 5.28 us -> 0.75 us  [per_device(): (residual.astype(jnp.float32) + attn.astype(jnp.float32)).astype(jnp.bflo...]
  transfers between devices with their start and end apart: 2 -> 0, of which waited for: 2 -> 0; matrix products, arithmetic and copies ran while one was open for 0% -> 0% of each run, Pallas kernels for 0% -> 0%
where the time goes in v1:
time: 105 us
  Pallas kernels  92.3 us (88%)
  matrix products  6.57 us (6%)
  local copies, waits for them, and re-layouts  3.17 us (3%)
  other arithmetic  2.51 us (2%)
    pallas_call x1, Pallas kernels, feed_forward(): pl.pallas_call(feed_forward_kernel, out_shape=jax.ShapeDtypeStruct((rows,...  92.3 us
    dot_general x1, matrix products, per_device(): jnp.einsum('rkgd,rkld->rkgl', query_heads, cached_key_rows, preferred_ele...  3.48 us
    dot_general x1, matrix products, per_device(): jnp.einsum('rkgl,rkld->rkgd', weights.astype(jnp.bfloat16), cached_value_...  2.9 us
    unnamed x14, local copies, waits for them, and re-layouts  2.54 us

profile of v1, /device:TPU:0, one launch (start us, length us, event | category | flops | bytes accessed | tf_op | source)
XLA Modules:
  0.0 104.7 jit_solution(15483454432745870714)
XLA Ops:
  0.0 0.0 copy-start.1
  0.0 0.0 copy-start.2
  0.0 0.9 copy.20
  0.9 0.7 iota_compare_fusion
  1.7 3.5 %fusion.10 = (f32[32,2,8]{2,1,0:T(2,128)S(1)}, f32[32,2,8,256]{3,2,1,0:T(8,128)S(1)}) fusion(bf16[32,2,8,128]{3,2,1,0:T(8,128)(2,1)S(1)} %bitcast.26, bf16[32,2,256,128]{3,2,1,0:T(8,128)(2,1)} %param.18, pred[32,256]{1,0:T(8,128)(4,1)S(1)} %iota_compare_fusion), kind=kOutput, calls=%fused_computation.18 | convolution fusion | flops 33947136 | bytes 4859904 | tf_op jit(solution)/shard_map/rkgd,rkld->rkgl/dot_general | solution.py:375
  5.2 0.0 copy-done.1
  5.2 0.0 copy-start
  5.2 0.2 fusion.11
  5.4 0.0 copy-start.3
  5.5 0.0 copy-start.4
  5.5 0.0 copy-start.5
  5.5 0.3 fusion.4
  5.8 0.0 copy-done.2
  5.9 2.9 %fusion.3 = f32[32,2,8,128]{3,2,1,0:T(8,128)S(1)} fusion(bf16[32,2,256,128]{3,2,1,0:T(8,128)(2,1)} %param.19, f32[32,2,8,256]{3,2,1,0:T(8,128)S(1)} %get-tuple-element.8, f32[32,2,8]{2,1,0:T(2,128)S(1)} %multiply_maximum_fusion, f32[32,2,8]{2,1,0:T(2,128)S(1)} %get-tuple-element.5, f32[32,2,128]{2,1,0:T(2,128)S(1)} %reshape.64, ...), kind=kOutput, calls=%fused_computation.5 | convolution fusion | flops 34144256 | bytes 5019648 | tf_op jit(solution)/shard_map/rkgl,rkld->rkgd/dot_general | solution.py:396
  8.8 0.0 copy-done
  8.8 0.8 fusion.7.stream_ref
  9.5 0.0 copy-done.3
  9.5 0.6 reshape.59.gain_ref
  10.1 0.0 copy-done.4
  10.1 0.0 copy-done.5
  10.1 0.7 select_reduce_fusion
  10.8 92.3 %shard_map.163 = bf16[32,2048]{1,0:T(8,128)(2,1)} custom-call(s32[1,128]{1,0:T(1,128)} %bitcast.33, bf16[32,2048]{1,0:T(8,128)(2,1)} %fusion.7.stream_ref, bf16[1,2048]{1,0:T(2,128)(2,1)} %reshape.59.gain_ref, bf16[128,2048]{1,0:T(8,128)(2,1)} %bitcast.24, bf16[128,4096]{1,0:T(8,128)(2,1)} %bitcast.23, bf16[256,1024]{1,0:T(8,128)(2,1)} %bitcast.25, ...), custom_call_target="tpu_custom_call" | custom-call | flops 6442450944 | bytes 50331648 | tf_op jit(solution)/shard_map/pallas_call | solution.py:305
  103.1 1.6 %copy.24 = bf16[32,2048]{1,0:T(8,128)(2,1)} copy(bf16[32,2048]{1,0:T(8,128)(2,1)} %shard_map.163) | data formatting | bytes 262144
  (4 shorter events, 0.1 us)
Async XLA Ops:
  0.0 5.2 %copy-start.1 = (bf16[32,256]{1,0:T(8,128)(2,1)S(1)}, bf16[32,256]{1,0:T(8,128)(2,1)}, u32[]{:S(2)}) copy-start(bf16[32,256]{1,0:T(8,128)(2,1)} %param.20) | copy-start | bytes 49156
  0.0 5.8 %copy-start.2 = (bf16[32,256]{1,0:T(8,128)(2,1)S(1)}, bf16[32,256]{1,0:T(8,128)(2,1)}, u32[]{:S(2)}) copy-start(bf16[32,256]{1,0:T(8,128)(2,1)} %param.21) | copy-start | bytes 49156
  5.2 3.6 %copy-start = (bf16[32,2048]{1,0:T(8,128)(2,1)S(1)}, bf16[32,2048]{1,0:T(8,128)(2,1)}, u32[]{:S(2)}) copy-start(bf16[32,2048]{1,0:T(8,128)(2,1)} %param.23) | copy-start | bytes 393220
  5.4 4.1 %copy-start.3 = (bf16[2048]{0:T(1024)(128)(2,1)S(1)}, bf16[2048]{0:T(1024)(128)(2,1)}, u32[]{:S(2)}) copy-start(bf16[2048]{0:T(1024)(128)(2,1)} %param.24) | copy-start | bytes 12292
  5.5 4.7 %copy-start.4 = (s32[16]{0:T(128)S(1)}, s32[16]{0:T(128)}, u32[]{:S(2)}) copy-start(s32[16]{0:T(128)} %param.33) | copy-start | bytes 196
  5.5 4.7 %copy-start.5 = (s32[128]{0:T(128)S(1)}, s32[128]{0:T(128)}, u32[]{:S(2)}) copy-start(s32[128]{0:T(128)} %param.32) | copy-start | bytes 1540

commit v2 on v1

--- a/solution.py
+++ b/solution.py
@@ -13,7 +13,7 @@
 
 
 def feed_forward_kernel(
-    slot_ref, stream_ref, gain_ref, ain_hbm, omap_hbm, dai_hbm, dout_hbm, gate_hbm, up_hbm, down_hbm,
+    storage_ref, request_ref, stream_ref, gain_ref, ain_hbm, omap_hbm, dai_hbm, dout_hbm, gate_hbm, up_hbm, down_hbm,
     out_ref,
     raw, x, ain, omap, dai, dout, w, dw,
     ex_send, ex_recv, pf, s1_send, s1_recv, fwd, own, s2_send, s2_recv,
@@ -80,17 +80,20 @@
     def raw_copy(owner, d, dev):
         return remote(raw.at[owner], raw.at[owner], raw_ss.at[d - 1], raw_rs.at[owner], dev, z)
 
-    for d in (1, 2, 3):
-        raw_copy(me_w, d, lax.rem(me_w + d, 4)).start()
+    across = lax.rem(me_w + 2, 4)
+    sibling = me_w + 1 - 2 * lax.rem(me_w, 2)
+    raw_copy(me_w, 1, across).start()
+    raw_copy(me_w, 2, sibling).start()
 
     def dw_start(k, carry):
         dw_copy(k).start()
         return carry
 
     lax.fori_loop(0, 16, dw_start, 0)
-    for d in (1, 2, 3):
-        peer = lax.rem(me_w + d, 4)
-        raw_copy(peer, d, peer).wait_recv()
+    raw_copy(across, 1, across).wait_recv()
+    raw_copy(across, 3, sibling).start()
+    raw_copy(sibling, 2, sibling).wait_recv()
+    raw_copy(lax.rem(sibling + 2, 4), 3, sibling).wait_recv()
     gain = gain_ref[...].astype(f32)
     squares = []
     for p in range(4):
@@ -99,7 +102,9 @@
         x[pl.ds(p * rows, rows), :] = (part * gain).astype(bf16)
     square = jnp.broadcast_to(jnp.concatenate(squares, axis=0), (total, total)).T
 
-    slot_row = slot_ref[...]
+    slot_row = jnp.zeros((1, total), jnp.int32)
+    for a in range(16):
+        slot_row = slot_row + jnp.where(request_ref[...] == a, storage_ref[a], 0)
     small_copy(0).wait()
     inner = lax.dot_general(ain[...], x[...], NT, preferred_element_type=f32)
     chosen = jnp.zeros((32, total), f32)
@@ -163,6 +168,43 @@
         s2_send[b] = (fwd[b] + s1_recv[0, b].astype(f32)).astype(bf16)
         s2_copy(b).start()
 
+    def h_copy(q, b, d, dev):
+        return remote(hid.at[q, b], hid.at[q, b], h_ss.at[d - 1, b], h_rs.at[q, b], me_w, dev)
+
+    def add_product(q, b):
+        k = q * 4 + b
+        dw_copy(k).wait()
+        acc[...] += jnp.dot(hid[q, b], dw[k], preferred_element_type=f32)
+
+    def add_others(b):
+        for d in (1, 2, 3):
+            q = quarters[3 - d]
+            h_copy(q, b, d, q).wait_recv()
+            add_product(q, b)
+
+    acc[...] = jnp.zeros_like(acc)
+    dinner[...] = jnp.zeros_like(dinner)
+    small_copy(2).wait()
+
+    def finish(b, carry):
+        s1_copy(1, b).wait_recv()
+        s2_copy(b).wait_recv()
+        value = own[b] + s1_recv[1, b].astype(f32) + s2_recv[b].astype(f32)
+        gate = value[:, :sub] * scale
+        up = value[:, sub:] * scale
+        hid[z, b] = (gate / (1.0 + jnp.exp(-gate)) * up).astype(bf16)
+        for d in (3, 2, 1):
+            h_copy(z, b, d, quarters[3 - d]).start()
+        dinner[...] += lax.dot_general(
+            dai[:, pl.ds(pl.multiple_of(b * sub, sub), sub)], hid[z, b], NT, preferred_element_type=f32)
+        add_product(z, b)
+
+        @pl.when(b > 0)
+        def _():
+            add_others(b - 1)
+
+        return carry
+
     def spread(b, carry):
         for i in range(4):
             term = jnp.dot(placed, omap[:, pl.ds(column(quarters[i], b), sub)], preferred_element_type=f32)
@@ -184,49 +226,16 @@
         def _():
             pass_on(b - 1)
 
+        @pl.when(b > 1)
+        def _():
+            finish(b - 2, 0)
+
         return carry
 
     lax.fori_loop(0, 4, spread, 0)
     pass_on(jnp.int32(3))
-
-    def h_copy(q, b, d, dev):
-        return remote(hid.at[q, b], hid.at[q, b], h_ss.at[d - 1, b], h_rs.at[q, b], me_w, dev)
-
-    def add_product(q, b):
-        k = q * 4 + b
-        dw_copy(k).wait()
-        acc[...] += jnp.dot(hid[q, b], dw[k], preferred_element_type=f32)
-
-    def add_others(b):
-        for d in (1, 2, 3):
-            q = quarters[3 - d]
-            h_copy(q, b, d, q).wait_recv()
-            add_product(q, b)
-
-    acc[...] = jnp.zeros_like(acc)
-    dinner[...] = jnp.zeros_like(dinner)
-    small_copy(2).wait()
-
-    def finish(b, carry):
-        s1_copy(1, b).wait_recv()
-        s2_copy(b).wait_recv()
-        value = own[b] + s1_recv[1, b].astype(f32) + s2_recv[b].astype(f32)
-        gate = value[:, :sub] * scale
-        up = value[:, sub:] * scale
-        hid[z, b] = (gate / (1.0 + jnp.exp(-gate)) * up).astype(bf16)
-        for d in (3, 2, 1):
-            h_copy(z, b, d, quarters[3 - d]).start()
-        dinner[...] += lax.dot_general(
-            dai[:, pl.ds(pl.multiple_of(b * sub, sub), sub)], hid[z, b], NT, preferred_element_type=f32)
-        add_product(z, b)
-
-        @pl.when(b > 0)
-        def _():
-            add_others(b - 1)
-
-        return carry
-
-    lax.fori_loop(0, 4, finish, 0)
+    finish(jnp.int32(2), 0)
+    finish(jnp.int32(3), 0)
 
     down_low = jnp.zeros((16, total), f32)
     for a in range(16):
@@ -288,7 +297,7 @@
     lax.fori_loop(0, 4, drain, 0)
 
 
-def feed_forward(stream, norm_gain, gate, up, down, ain, omaps, dai, dout, slot_of_row):
+def feed_forward(stream, norm_gain, gate, up, down, ain, omaps, dai, dout, request, storage):
     rows, width = stream.shape
     total = 4 * rows
     hidden = gate.shape[1]
@@ -305,7 +314,7 @@
     return pl.pallas_call(
         feed_forward_kernel,
         out_shape=jax.ShapeDtypeStruct((rows, width), bf16),
-        in_specs=[vmem] * 3 + [hbm] * 7,
+        in_specs=[pl.BlockSpec(memory_space=pltpu.SMEM)] + [vmem] * 3 + [hbm] * 7,
         out_specs=vmem,
         scratch_shapes=[
             pltpu.VMEM((4, rows, width), bf16),
@@ -341,7 +350,7 @@
             collective_id=0, has_side_effects=True, vmem_limit_bytes=58 * 2**20),
         cost_estimate=pl.CostEstimate(
             flops=6 * total * width * hidden, bytes_accessed=6 * width * hidden, transcendentals=0),
-    )(slot_of_row.reshape(1, total), stream, norm_gain.reshape(1, width), ain_t, omap, dai2, dout2,
+    )(storage, request.reshape(1, total), stream, norm_gain.reshape(1, width), ain_t, omap, dai2, dout2,
       gate, up, down)
 
 
@@ -403,12 +412,6 @@
     attn = (mixed / denominator[..., None]).reshape(rows_here, -1).astype(jnp.bfloat16)
     stream = (residual.astype(jnp.float32) + attn.astype(jnp.float32)).astype(jnp.bfloat16)
     if lax.axis_size("tp") == 4 and lax.axis_size("wide") == 4 and rows_here == 32:
-        ids = lax.broadcasted_iota(
-            jnp.int32, (request_adapter.shape[0], adapter_storage_slot.shape[0]), 1
-        )
-        slots = jnp.sum(
-            jnp.where(request_adapter[:, None] == ids, adapter_storage_slot[None, :], 0), axis=1
-        )
         return feed_forward(
             stream,
             norm_gain_vector,
@@ -419,7 +422,8 @@
             adapter_output_maps,
             down_adapter_input,
             down_adapter_output,
-            slots,
+            request_adapter,
+            adapter_storage_slot,
         )
     tp_count = lax.axis_size("tp")
     my_tp = lax.axis_index("tp")

time: 105 us -> 100 us (0.952)
  Pallas kernels: 92.3 us -> 88.2 us
    pallas_call x1, Pallas kernels: 92.3 us -> 88.2 us  [feed_forward(): pl.pallas_call(feed_forward_kernel, out_shape=jax.ShapeDtypeStruct((rows,...]
    unnamed x14 -> x10, local copies, waits for them, and re-layouts: 2.54 us -> 2.53 us
where the time goes in v2:
time: 100 us; the launch traced here: 99.9 us
  Pallas kernels  88.2 us (88%)
  matrix products  6.57 us (7%)
  local copies, waits for them, and re-layouts  3.16 us (3%)
  other arithmetic  1.84 us (2%)
    pallas_call x1, Pallas kernels, feed_forward(): pl.pallas_call(feed_forward_kernel, out_shape=jax.ShapeDtypeStruct((rows,...  88.2 us
    dot_general x1, matrix products, per_device(): jnp.einsum('rkgd,rkld->rkgl', query_heads, cached_key_rows, preferred_ele...  3.48 us
    dot_general x1, matrix products, per_device(): jnp.einsum('rkgl,rkld->rkgd', weights.astype(jnp.bfloat16), cached_value_...  2.9 us
    unnamed x10, local copies, waits for them, and re-layouts  2.53 us

profile of v2, /device:TPU:0, one launch (start us, length us, event | category | flops | bytes accessed | tf_op | source)
XLA Modules:
  0.0 99.9 jit_solution(10758907160113491941)
XLA Ops:
  0.0 0.0 copy-start.1
  0.0 0.0 copy-start.2
  0.0 0.9 copy.20
  0.9 0.7 iota_compare_fusion
  1.7 3.5 %fusion.10 = (f32[32,2,8]{2,1,0:T(2,128)S(1)}, f32[32,2,8,256]{3,2,1,0:T(8,128)S(1)}) fusion(bf16[32,2,8,128]{3,2,1,0:T(8,128)(2,1)S(1)} %bitcast.26, bf16[32,2,256,128]{3,2,1,0:T(8,128)(2,1)} %param.18, pred[32,256]{1,0:T(8,128)(4,1)S(1)} %iota_compare_fusion), kind=kOutput, calls=%fused_computation.16 | convolution fusion | flops 33947136 | bytes 4859904 | tf_op jit(solution)/shard_map/rkgd,rkld->rkgl/dot_general | solution.py:384
  5.2 0.0 copy-done.1
  5.2 0.0 copy-start
  5.2 0.2 fusion.11
  5.4 0.0 copy-start.3
  5.5 0.3 fusion.4
  5.8 0.0 copy-done.2
  5.8 2.9 %fusion.3 = f32[32,2,8,128]{3,2,1,0:T(8,128)S(1)} fusion(bf16[32,2,256,128]{3,2,1,0:T(8,128)(2,1)} %param.19, f32[32,2,8,256]{3,2,1,0:T(8,128)S(1)} %get-tuple-element.8, f32[32,2,8]{2,1,0:T(2,128)S(1)} %multiply_maximum_fusion, f32[32,2,8]{2,1,0:T(2,128)S(1)} %get-tuple-element.5, f32[32,2,128]{2,1,0:T(2,128)S(1)} %reshape.62, ...), kind=kOutput, calls=%fused_computation.5 | convolution fusion | flops 34144256 | bytes 5019648 | tf_op jit(solution)/shard_map/rkgl,rkld->rkgd/dot_general | solution.py:405
  8.7 0.0 copy-done
  8.7 0.8 fusion.7.stream_ref
  9.5 0.0 copy-done.3
  9.5 0.6 reshape.57.gain_ref
  10.1 88.2 %shard_map.163 = bf16[32,2048]{1,0:T(8,128)(2,1)} custom-call(s32[16]{0:T(128)} %storage_ref.1, s32[1,128]{1,0:T(1,128)} %bitcast.33, bf16[32,2048]{1,0:T(8,128)(2,1)} %fusion.7.stream_ref, bf16[1,2048]{1,0:T(2,128)(2,1)} %reshape.57.gain_ref, bf16[128,2048]{1,0:T(8,128)(2,1)} %bitcast.24, bf16[128,4096]{1,0:T(8,128)(2,1)} %bitcast.23, ...), custom_call_target="tpu_custom_call" | custom-call | flops 6442450944 | bytes 50331648 | tf_op jit(solution)/shard_map/pallas_call | solution.py:314
  98.3 1.6 %copy.24 = bf16[32,2048]{1,0:T(8,128)(2,1)} copy(bf16[32,2048]{1,0:T(8,128)(2,1)} %shard_map.163) | data formatting | bytes 262144
  (4 shorter events, 0.1 us)
Async XLA Ops:
  0.0 5.2 %copy-start.1 = (bf16[32,256]{1,0:T(8,128)(2,1)S(1)}, bf16[32,256]{1,0:T(8,128)(2,1)}, u32[]{:S(2)}) copy-start(bf16[32,256]{1,0:T(8,128)(2,1)} %param.20) | copy-start | bytes 49156
  0.0 5.8 %copy-start.2 = (bf16[32,256]{1,0:T(8,128)(2,1)S(1)}, bf16[32,256]{1,0:T(8,128)(2,1)}, u32[]{:S(2)}) copy-start(bf16[32,256]{1,0:T(8,128)(2,1)} %param.21) | copy-start | bytes 49156
  5.2 3.5 %copy-start = (bf16[32,2048]{1,0:T(8,128)(2,1)S(1)}, bf16[32,2048]{1,0:T(8,128)(2,1)}, u32[]{:S(2)}) copy-start(bf16[32,2048]{1,0:T(8,128)(2,1)} %param.23) | copy-start | bytes 393220
  5.4 4.1 %copy-start.3 = (bf16[2048]{0:T(1024)(128)(2,1)S(1)}, bf16[2048]{0:T(1024)(128)(2,1)}, u32[]{:S(2)}) copy-start(bf16[2048]{0:T(1024)(128)(2,1)} %param.24) | copy-start | bytes 12292

commit v3 on v2

--- a/solution.py
+++ b/solution.py
@@ -15,7 +15,7 @@
 def feed_forward_kernel(
     storage_ref, request_ref, stream_ref, gain_ref, ain_hbm, omap_hbm, dai_hbm, dout_hbm, gate_hbm, up_hbm, down_hbm,
     out_ref,
-    raw, x, ain, omap, dai, dout, w, dw,
+    raw, squares, x, ain, omap, dai, dout, w, dw,
     ex_send, ex_recv, pf, s1_send, s1_recv, fwd, own, s2_send, s2_recv,
     hid, dinner, dx_send, dx_recv, acc, o_send, o_recv,
     small_sem, w_sem, dw_sem,
@@ -90,17 +90,24 @@
         return carry
 
     lax.fori_loop(0, 16, dw_start, 0)
+    gain = gain_ref[...].astype(f32)
+
+    def prepare(p):
+        part = raw[p].astype(f32)
+        here = pl.ds(pl.multiple_of(p * rows, rows), rows)
+        squares[here, :] = jnp.broadcast_to(jnp.sum(part * part, axis=1, keepdims=True), (rows, total))
+        x[here, :] = (part * gain).astype(bf16)
+
+    prepare(me_w)
     raw_copy(across, 1, across).wait_recv()
     raw_copy(across, 3, sibling).start()
     raw_copy(sibling, 2, sibling).wait_recv()
-    raw_copy(lax.rem(sibling + 2, 4), 3, sibling).wait_recv()
-    gain = gain_ref[...].astype(f32)
-    squares = []
-    for p in range(4):
-        part = raw[p].astype(f32)
-        squares.append(jnp.sum(part * part, axis=1, keepdims=True))
-        x[pl.ds(p * rows, rows), :] = (part * gain).astype(bf16)
-    square = jnp.broadcast_to(jnp.concatenate(squares, axis=0), (total, total)).T
+    prepare(sibling)
+    prepare(across)
+    diagonal = lax.rem(sibling + 2, 4)
+    raw_copy(diagonal, 3, sibling).wait_recv()
+    prepare(diagonal)
+    square = squares[...].T
 
     slot_row = jnp.zeros((1, total), jnp.int32)
     for a in range(16):
@@ -186,7 +193,22 @@
     dinner[...] = jnp.zeros_like(dinner)
     small_copy(2).wait()
 
-    def finish(b, carry):
+    def dx_copy(owner, e, peer):
+        return remote(dx_send, dx_recv.at[owner], dx_ss.at[e], dx_rs.at[owner], peer // 4, lax.rem(peer, 4))
+
+    def dx_start(e, carry):
+        dx_copy(me, e, lax.rem(me + e, 16)).start()
+        return carry
+
+    def send_low():
+        down_low = jnp.zeros((16, total), f32)
+        for a in range(16):
+            down_low = down_low + jnp.where(slot_row == a, dinner[a * 16:(a + 1) * 16, :], 0.0)
+        dx_send[...] = down_low
+        dx_recv[me] = down_low
+        lax.fori_loop(1, 16, dx_start, 0)
+
+    def finish(b, last):
         s1_copy(1, b).wait_recv()
         s2_copy(b).wait_recv()
         value = own[b] + s1_recv[1, b].astype(f32) + s2_recv[b].astype(f32)
@@ -197,13 +219,14 @@
             h_copy(z, b, d, quarters[3 - d]).start()
         dinner[...] += lax.dot_general(
             dai[:, pl.ds(pl.multiple_of(b * sub, sub), sub)], hid[z, b], NT, preferred_element_type=f32)
+        if last:
+            send_low()
         add_product(z, b)
 
         @pl.when(b > 0)
         def _():
             add_others(b - 1)
 
-        return carry
 
     def spread(b, carry):
         for i in range(4):
@@ -228,29 +251,15 @@
 
         @pl.when(b > 1)
         def _():
-            finish(b - 2, 0)
+            finish(b - 2, False)
 
         return carry
 
     lax.fori_loop(0, 4, spread, 0)
     pass_on(jnp.int32(3))
-    finish(jnp.int32(2), 0)
-    finish(jnp.int32(3), 0)
-
-    down_low = jnp.zeros((16, total), f32)
-    for a in range(16):
-        down_low = down_low + jnp.where(slot_row == a, dinner[a * 16:(a + 1) * 16, :], 0.0)
-    dx_send[...] = down_low
-    dx_recv[me] = down_low
-
-    def dx_copy(owner, e, peer):
-        return remote(dx_send, dx_recv.at[owner], dx_ss.at[e], dx_rs.at[owner], peer // 4, lax.rem(peer, 4))
-
-    def dx_start(e, carry):
-        dx_copy(me, e, lax.rem(me + e, 16)).start()
-        return carry
-
-    lax.fori_loop(1, 16, dx_start, 0)
+    finish(jnp.int32(2), False)
+    finish(jnp.int32(3), True)
+
     add_others(jnp.int32(3))
 
     def dx_wait(e, carry):
@@ -318,6 +327,7 @@
         out_specs=vmem,
         scratch_shapes=[
             pltpu.VMEM((4, rows, width), bf16),
+            pltpu.VMEM((total, total), f32),
             pltpu.VMEM((total, width), bf16),
             pltpu.VMEM(ain_t.shape, bf16),
             pltpu.VMEM(omap.shape, bf16),

time: 100 us -> 99.9 us (level)
  no operation moved by 1% of the time
where the time goes in v3:
time: 99.9 us; the launch traced here: 99.7 us
  Pallas kernels  88 us (88%)
  matrix products  6.57 us (7%)
  local copies, waits for them, and re-layouts  3.16 us (3%)
  other arithmetic  1.84 us (2%)
    pallas_call x1, Pallas kernels, feed_forward(): pl.pallas_call(feed_forward_kernel, out_shape=jax.ShapeDtypeStruct((rows,...  88 us
    dot_general x1, matrix products, per_device(): jnp.einsum('rkgd,rkld->rkgl', query_heads, cached_key_rows, preferred_ele...  3.48 us
    dot_general x1, matrix products, per_device(): jnp.einsum('rkgl,rkld->rkgd', weights.astype(jnp.bfloat16), cached_value_...  2.9 us
    unnamed x10, local copies, waits for them, and re-layouts  2.53 us

profile of v3, /device:TPU:0, one launch (start us, length us, event | category | flops | bytes accessed | tf_op | source)
XLA Modules:
  0.0 99.7 jit_solution(6286022698345802903)
XLA Ops:
  0.0 0.0 copy-start.1
  0.0 0.0 copy-start.2
  0.0 0.9 copy.20
  0.9 0.7 iota_compare_fusion
  1.7 3.5 %fusion.10 = (f32[32,2,8]{2,1,0:T(2,128)S(1)}, f32[32,2,8,256]{3,2,1,0:T(8,128)S(1)}) fusion(bf16[32,2,8,128]{3,2,1,0:T(8,128)(2,1)S(1)} %bitcast.26, bf16[32,2,256,128]{3,2,1,0:T(8,128)(2,1)} %param.18, pred[32,256]{1,0:T(8,128)(4,1)S(1)} %iota_compare_fusion), kind=kOutput, calls=%fused_computation.16 | convolution fusion | flops 33947136 | bytes 4859904 | tf_op jit(solution)/shard_map/rkgd,rkld->rkgl/dot_general | solution.py:394
  5.2 0.0 copy-done.1
  5.2 0.0 copy-start
  5.2 0.2 fusion.11
  5.4 0.0 copy-start.3
  5.5 0.3 fusion.4
  5.8 0.0 copy-done.2
  5.8 2.9 %fusion.3 = f32[32,2,8,128]{3,2,1,0:T(8,128)S(1)} fusion(bf16[32,2,256,128]{3,2,1,0:T(8,128)(2,1)} %param.19, f32[32,2,8,256]{3,2,1,0:T(8,128)S(1)} %get-tuple-element.8, f32[32,2,8]{2,1,0:T(2,128)S(1)} %multiply_maximum_fusion, f32[32,2,8]{2,1,0:T(2,128)S(1)} %get-tuple-element.5, f32[32,2,128]{2,1,0:T(2,128)S(1)} %reshape.62, ...), kind=kOutput, calls=%fused_computation.5 | convolution fusion | flops 34144256 | bytes 5019648 | tf_op jit(solution)/shard_map/rkgl,rkld->rkgd/dot_general | solution.py:415
  8.7 0.0 copy-done
  8.7 0.8 fusion.7.stream_ref
  9.5 0.0 copy-done.3
  9.5 0.6 reshape.57.gain_ref
  10.1 88.0 %shard_map.163 = bf16[32,2048]{1,0:T(8,128)(2,1)} custom-call(s32[16]{0:T(128)} %storage_ref.1, s32[1,128]{1,0:T(1,128)} %bitcast.33, bf16[32,2048]{1,0:T(8,128)(2,1)} %fusion.7.stream_ref, bf16[1,2048]{1,0:T(2,128)(2,1)} %reshape.57.gain_ref, bf16[128,2048]{1,0:T(8,128)(2,1)} %bitcast.24, bf16[128,4096]{1,0:T(8,128)(2,1)} %bitcast.23, ...), custom_call_target="tpu_custom_call" | custom-call | flops 6442450944 | bytes 50331648 | tf_op jit(solution)/shard_map/pallas_call | solution.py:323
  98.1 1.6 %copy.24 = bf16[32,2048]{1,0:T(8,128)(2,1)} copy(bf16[32,2048]{1,0:T(8,128)(2,1)} %shard_map.163) | data formatting | bytes 262144
  (4 shorter events, 0.1 us)
Async XLA Ops:
  0.0 5.2 %copy-start.1 = (bf16[32,256]{1,0:T(8,128)(2,1)S(1)}, bf16[32,256]{1,0:T(8,128)(2,1)}, u32[]{:S(2)}) copy-start(bf16[32,256]{1,0:T(8,128)(2,1)} %param.20) | copy-start | bytes 49156
  0.0 5.8 %copy-start.2 = (bf16[32,256]{1,0:T(8,128)(2,1)S(1)}, bf16[32,256]{1,0:T(8,128)(2,1)}, u32[]{:S(2)}) copy-start(bf16[32,256]{1,0:T(8,128)(2,1)} %param.21) | copy-start | bytes 49156
  5.2 3.5 %copy-start = (bf16[32,2048]{1,0:T(8,128)(2,1)S(1)}, bf16[32,2048]{1,0:T(8,128)(2,1)}, u32[]{:S(2)}) copy-start(bf16[32,2048]{1,0:T(8,128)(2,1)} %param.23) | copy-start | bytes 393220
  5.4 4.1 %copy-start.3 = (bf16[2048]{0:T(1024)(128)(2,1)S(1)}, bf16[2048]{0:T(1024)(128)(2,1)}, u32[]{:S(2)}) copy-start(bf16[2048]{0:T(1024)(128)(2,1)} %param.24) | copy-start | bytes 12292
